TPU v7x, 128 devices: a whole 4x4x4 slice. The times are simulated.
128 devices in a mesh: gx: 8 (over x, core), gy: 4 (over y), gz: 4 (over z).
Axes of the slice: x: 4, y: 4, z: 4, core: 2. Of those that a mesh axis runs over, the one named last changes fastest.
Arguments:
- field: bfloat16 [64, 32, 32, 512], P(None, 'gx', 'gy', 'gz'), may hold values from -6 to 6
- cotangent: bfloat16 [64, 32, 32, 512], P(None, 'gx', 'gy', 'gz'), may hold values from -6 to 6
- w_fine: bfloat16 [3, 3, 3, 64, 64], replicated, may hold values from -0.15625 to 0.15625
- w_down: bfloat16 [2, 2, 2, 64, 64], replicated, may hold values from -0.25 to 0.25
- w_coarse: bfloat16 [3, 3, 3, 64, 64], replicated, may hold values from -0.15625 to 0.15625
- w_up: bfloat16 [2, 2, 2, 64, 64], replicated, may hold values from -0.75 to 0.75
Outputs:
- grad_field: bfloat16 [64, 32, 32, 512], P(None, 'gx', 'gy', 'gz')
- grad_fine: float32 [3, 3, 3, 64, 64], replicated
- grad_down: float32 [2, 2, 2, 64, 64], replicated
- grad_coarse: float32 [3, 3, 3, 64, 64], replicated
- grad_up: float32 [2, 2, 2, 64, 64], replicated
All inputs are finite; a program needn't handle non-finite values.
Results may differ from a plain program's by a relative error of at most 0.008.
Values may be sent and summed in bfloat16 or wider, within the bound.
A program may use at most 64 MiB of HBM per device.

v0:
```python
import functools

import jax
import jax.numpy as jnp
from jax import lax
from jax.experimental import pallas as pl
from jax.experimental.pallas import tpu as pltpu
from jax.sharding import PartitionSpec as P

MESH = pl.DeviceIdType.MESH
F32 = jnp.float32
BF16 = jnp.bfloat16
C = 64
Z = 128
NEG = 0.2

FLAT = [(dx, dy) for dx in (0, 1, -1) for dy in (0, 1, -1)]

SIDES = [(1, 0, 0), (-1, 0, 0)] + [(dx, dy, 0) for dx in (1, -1, 0) for dy in (1, -1)]
ENDS = [(dx, dy, dz) for dx, dy in FLAT[::-1] for dz in (1, -1)]


def act_slope(z):
    e = jnp.exp(-jnp.abs(z))
    q = 1.0 / (1.0 + e)
    sig = jnp.where(z >= 0.0, q, e * q)
    soft = jnp.maximum(z, 0.0) + jnp.log(1.0 + e)
    return NEG * z + (1.0 - NEG) * soft, NEG + (1.0 - NEG) * sig


def dot(a, b):
    return lax.dot_general(a, b, (((1,), (0,)), ((), ())), preferred_element_type=F32)


def dot_nt(a, b):
    return lax.dot_general(a, b, (((1,), (1,)), ((), ())), preferred_element_type=F32)


def roll(v, shift):
    shift = shift % Z
    return v if shift == 0 else pltpu.roll(v, shift, 1)


def lanes(rows):
    return lax.broadcasted_iota(jnp.int32, (rows, Z), 1)


class Level:
    def __init__(self, nx, ny, step, wide):
        self.nx, self.ny, self.step = nx, ny, step
        self.wide = wide

    def at(self, y, x):
        return self.wide * y + x


def put_own(level, v_ref, y, x, pencil):
    v_ref[y + 1, x, C : 2 * C, :] = pencil
    if x + 1 < level.nx:
        v_ref[y + 1, x + 1, 0:C, :] = pencil
    if x >= 1:
        v_ref[y + 1, x - 1, 2 * C : 3 * C, :] = pencil


def spread_y_halo(level, v_ref):
    for y in (0, level.ny + 1):
        for x in range(level.nx):
            if x + 1 < level.nx:
                v_ref[y, x + 1, 0:C, :] = v_ref[y, x, C : 2 * C, :]
            if x >= 1:
                v_ref[y, x - 1, 2 * C : 3 * C, :] = v_ref[y, x, C : 2 * C, :]


def add_face(level, face, y, x, pencil):
    spot = level.at(y + 1, x + 1)
    return jnp.where(lanes(C) // 2 == spot, roll(pencil, 2 * spot + 1), face)


def pack_face(face, z_send):
    odd = lanes(C // 2) % 2 == 1
    top, bottom = face[: C // 2], face[C // 2 :]
    z_send[0] = jnp.where(odd, top, roll(bottom, -1)).astype(BF16)
    z_send[1] = jnp.where(odd, roll(bottom, 1), top).astype(BF16)


def planes(level, z_recv):
    lane = lanes(C // 2)
    spot = lane // 2
    at_y, at_x = spot // level.wide, spot % level.wide

    def side(value, size, d):
        if d == 1:
            return value == 0
        if d == -1:
            return value == size + 1
        return (value >= 1) & (value <= size)

    packed = []
    for which in range(2):
        total = jnp.zeros((C // 2, Z), F32)
        for n, (dx, dy) in enumerate(FLAT):
            shift = -(level.nx * dx) - level.wide * level.ny * dy
            piece = roll(z_recv[n, which].astype(F32), 2 * shift)
            total = jnp.where(side(at_y, level.ny, dy) & side(at_x, level.nx, dx), piece, total)
        packed.append(total)
    low, high = packed
    odd = lane % 2 == 1
    top = jnp.where(odd, roll(low, 1), roll(high, -1))
    bottom = jnp.where(odd, low, high)
    return jnp.concatenate([top, bottom], axis=0)


def pack_ends(near, far, z_send):
    odd = lanes(C) % 2 == 1
    left = lanes(C // 2) < C
    down = jnp.where(odd, far, roll(near, -1))
    up = jnp.where(odd, roll(far, 1), near)
    for n, value in enumerate((down, up)):
        packed = jnp.where(left, value[: C // 2], roll(value[C // 2 :], C))
        z_send[n] = packed.astype(BF16)


def outer_planes(z_recv):
    lane = lanes(C)
    spot = lane // 2
    at_y, at_x = spot // 6, spot % 6
    sides = []
    for which in range(2):
        total = jnp.zeros((C, Z), F32)
        for n, (dx, dy) in enumerate(FLAT):
            first_y, last_y = {0: (2, 5), 1: (0, 1), -1: (6, 7)}[dy]
            first_x = 2 - 2 * dx
            mine = (at_y >= first_y) & (at_y <= last_y) & (at_x >= first_x) & (at_x <= first_x + 1)
            packed = z_recv[n, which].astype(F32)
            value = jnp.concatenate([packed, roll(packed, C)], axis=0)
            total = jnp.where(mine, roll(value, 2 * (14 - 2 * dx - 24 * dy)), total)
        sides.append(total)
    low, high = sides
    odd = lane % 2 == 1
    return jnp.where(odd, roll(low, 1), high), jnp.where(odd, low, roll(high, -1))


def halo_columns(level, plane):
    return jnp.concatenate(
        [roll(plane, -2 * (a + level.wide * b)).astype(BF16) for b in range(3) for a in range(3)],
        axis=0,
    )


def stacked(level, v_ref, y, cols=None):
    return jnp.concatenate(
        [
            jnp.concatenate(
                [v_ref[y + b, x] for x in (range(level.nx) if cols is None else cols)], axis=1
            )
            for b in range(3)
        ],
        axis=0,
    )


def correction(weight, columns):
    p = dot(weight, columns)
    return jnp.where(lanes(C) % 2 == 1, p[:C], p[2 * C :])


def conv_rows(level, weight, v_ref, z_ref, beyond=None, rows=None, cols=None):
    lane = lanes(C)
    cols = range(level.nx) if cols is None else cols
    for y in range(level.ny) if rows is None else rows:
        p = dot(weight, stacked(level, v_ref, y, cols))
        for n, x in enumerate(cols):
            part = p[:, n * Z : (n + 1) * Z]
            left = jnp.where(lane < level.step, 0.0, roll(part[:C], level.step))
            right = jnp.where(lane >= Z - level.step, 0.0, roll(part[2 * C :], -level.step))
            z_ref[y, x] = part[C : 2 * C] + left + right
            if beyond is not None:
                spot = level.at(y, x)
                low = roll(part[2 * C :], 2 * spot + 1)
                high = roll(part[:C], 2 * spot - Z + level.step)
                beyond = jnp.where(lane == 2 * spot + 1, low, beyond)
                beyond = jnp.where(lane == 2 * spot, high, beyond)
    return beyond


def fixed(level, fix, z_ref, y, x):
    lane = lanes(C)
    spot = level.at(y, x)
    share = jnp.where(lane == 0, roll(fix, -(2 * spot + 1)), 0.0)
    share = jnp.where(lane == Z - level.step, roll(fix, -level.step - 2 * spot), share)
    return z_ref[y, x] + share


def taps_along_z(level, grad):
    lane = lanes(C)
    first = jnp.where(lane < Z - level.step, roll(grad, -level.step), 0.0)
    last = jnp.where(lane >= level.step, roll(grad, level.step), 0.0)
    return jnp.concatenate([first, grad, last], axis=0).astype(BF16)


def filter_sum(level, g_ref, face, v_ref, columns):
    lane = lanes(C)
    own = roll(face, -2 * (level.wide + 1))
    none = jnp.zeros((C, Z), F32)
    edge = jnp.concatenate(
        [jnp.where(lane % 2 == 1, own, 0.0), none, jnp.where(lane % 2 == 0, own, 0.0)], axis=0
    ).astype(BF16)
    spots = [(y, x) for y in range(level.ny) for x in range(level.nx)]
    grads = jnp.concatenate([g_ref[y, x] for y, x in spots] + [edge], axis=1)
    sums = []
    for b in range(3):
        ends = columns[b * 3 * C : (b + 1) * 3 * C]
        inputs = jnp.concatenate([v_ref[y + b, x] for y, x in spots] + [ends], axis=1)
        sums.append(dot_nt(grads, inputs))
    return sums


def kernel(
    sizes,
    field_hbm, cot_hbm, wf_hbm, wd_hbm, wc_hbm, wu_hbm,
    out_ref, a_ref, b_ref,
    field_ref, cot_ref, wf_ref, wd_ref, wc_ref, wu_ref,
    w_ff, w_fb, w_cf, w_cb, w_d, w_dt, w_u,
    v_f, v_e, g_c, g_f, both, up_ext,
    zs, zr,
    turn, cot, hid, up_grad, slope_f, slope_d, shifted_f, shifted_c, h_two, g_two, z_f, z_c, z_e,
    s_a, s_b, ra_a, ra_b, rb_a, rb_b, rc_a, rc_b,
    local, side_send, side_recv, end_send, end_recv, sum_send, sum_recv,
):
    cx, cy, cz = sizes
    me = (lax.axis_index("gx"), lax.axis_index("gy"), lax.axis_index("gz"))
    fine, coarse, outer = Level(4, 8, 1, 6), Level(2, 4, 2, 6), Level(4, 6, 2, 6)

    def device(d):
        return tuple(lax.rem(m + (o % n), n) for m, o, n in zip(me, d, sizes))

    first = SIDES + [(0, 0, 1), (0, 0, -1)] + [(i, 0, 0) for i in range(3, cx - 2)]
    partners = sorted({tuple(o % n for o, n in zip(d, sizes)) for d in first})
    barrier = pltpu.get_barrier_semaphore()
    for d in partners:
        pl.semaphore_signal(barrier, inc=1, device_id=device(d), device_id_type=MESH)

    def load_in(src, dst, n):
        copy = pltpu.make_async_copy(src, dst, local.at[n])
        copy.start()
        return copy

    field_in = [load_in(field_hbm.at[:, x], field_ref.at[:, x], x) for x in range(4)]
    cot_in = load_in(cot_hbm, cot_ref, 4)
    w_in = [
        load_in(src, dst, 5 + n)
        for n, (src, dst) in enumerate(
            ((wf_hbm, wf_ref), (wu_hbm, wu_ref), (wd_hbm, wd_ref), (wc_hbm, wc_ref))
        )
    ]

    started = []

    def send(src, dst, send_sem, recv_sem, d):
        copy = pltpu.make_async_remote_copy(
            src_ref=src,
            dst_ref=dst,
            send_sem=send_sem,
            recv_sem=recv_sem,
            device_id=device(d),
            device_id_type=MESH,
        )
        copy.start()
        started.append(copy)
        return copy

    def arrive(copies):
        for copy in copies:
            copy.wait_recv()

    def send_sides(which, views):
        copies = []
        for n, (dx, dy, _) in enumerate(SIDES):
            src, dst = views(dx, dy)
            copies.append(
                send(src, dst, side_send.at[which, n], side_recv.at[which, n], (dx, dy, 0))
            )
        return copies

    def along_axis(size, depth, d):
        src = {0: pl.ds(depth, size), 1: pl.ds(size, depth), -1: pl.ds(depth, depth)}[d]
        dst = {0: pl.ds(depth, size), 1: pl.ds(0, depth), -1: pl.ds(size + depth, depth)}[d]
        return src, dst

    def fine_views(v_ref):
        def views(dx, dy):
            ys, yd = along_axis(8, 1, dy)
            xs = {0: pl.ds(0, 4), 1: pl.ds(3, 1), -1: pl.ds(0, 1)}[dx]
            xd = {0: pl.ds(0, 4), 1: pl.ds(0, 1), -1: pl.ds(3, 1)}[dx]
            rows = pl.ds({0: C, 1: 0, -1: 2 * C}[dx], C)
            return v_ref.at[ys, xs, pl.ds(C, C), :], v_ref.at[yd, xd, rows, :]

        return views

    def up_views(dx, dy):
        (ys, yd), (xs, xd) = along_axis(4, 1, dy), along_axis(2, 1, dx)
        return up_ext.at[ys, xs], up_ext.at[yd, xd]

    def down_views(dx, dy):
        ys, yd = along_axis(4, 2, dy)
        return both.at[ys, 1], both.at[yd, 1 - dx]

    def send_ends(which, some):
        copies = []
        for dx, dy, dz in some:
            n = ENDS.index((dx, dy, dz))
            side = 1 if dz == 1 else 0
            src = zs.at[which, side]
            dst = zr.at[which, FLAT.index((dx, dy)), 1 - side]
            copies.append(send(src, dst, end_send.at[which, n], end_recv.at[which, n], (dx, dy, dz)))
        return copies

    def forward_ends(which):
        copies = []
        for n, (dx, dy) in enumerate(FLAT):
            if n:
                src, dst = zr.at[which, 0], zr.at[which, n]
                copies.append(
                    send(src, dst, end_send.at[which, n], end_recv.at[which, n], (dx, dy, 0))
                )
        return copies

    face = jnp.zeros((C, Z), F32)
    for x in range(4):
        field_in[x].wait()
        turn[x] = field_ref[:, x].astype(F32).reshape(C * 8, Z)
        for y in range(8):
            pencil = turn[x, pl.ds(y, C, stride=8), :]
            put_own(fine, v_f, y, x, pencil.astype(BF16))
            face = add_face(fine, face, y, x, pencil)
    pack_face(face, zs.at[0])

    pl.semaphore_wait(barrier, len(partners))
    ends = send_ends(0, ENDS[-2:])
    sides = send_sides(0, fine_views(v_f))

    eye = (
        lax.broadcasted_iota(jnp.int32, (C, C), 0) == lax.broadcasted_iota(jnp.int32, (C, C), 1)
    ).astype(BF16)

    def flipped(w):
        return dot_nt(eye, w).astype(BF16)

    def layout_3(w_ref, forward, backward):
        for a in range(3):
            for b in range(3):
                for c in range(3):
                    w = w_ref[a, b, c]
                    m = b * 3 + a
                    forward[c * C : (c + 1) * C, m * C : (m + 1) * C] = w
                    m, k = 8 - m, 2 - c
                    backward[k * C : (k + 1) * C, m * C : (m + 1) * C] = flipped(w)

    for copy in w_in:
        copy.wait()
    layout_3(wf_ref, w_ff, w_fb)
    arrive(ends)
    forwards = forward_ends(0)
    layout_3(wc_ref, w_cf, w_cb)
    for a in range(2):
        for b in range(2):
            for c in range(2):
                m = b * 2 + a
                w = wd_ref[a, b, c]
                w_d[c * C : (c + 1) * C, m * C : (m + 1) * C] = w
                w_dt[m * C : (m + 1) * C, c * C : (c + 1) * C] = flipped(w)
                w_u[c * C : (c + 1) * C, m * C : (m + 1) * C] = flipped(wu_ref[a, b, c])

    def pair(ref, y):
        return jnp.concatenate([ref[y, 0], ref[y, 1]], axis=1)

    cot_in.wait()
    for x in range(4):
        turn[x] = cot_ref[:, x].astype(F32).reshape(C * 8, Z)
        for y in range(8):
            m = (y % 2) * 2 + x % 2
            pencil = turn[x, pl.ds(y, C, stride=8), :]
            cot[y // 2, x // 2, m * C : (m + 1) * C, :] = pencil.astype(BF16)
    even = lanes(C) % 2 == 0
    odd = lanes(C) % 2 == 1
    face = jnp.zeros((C, Z), F32)
    for y in range(4):
        p = dot(w_u[...], pair(cot, y))
        for x in range(2):
            part = p[:, x * Z : (x + 1) * Z]
            g = part[:C] + roll(part[C:], -1)
            up_grad[y, x] = g
            up_ext[y + 1, x + 1] = g.astype(BF16)
            face = add_face(coarse, face, y, x, jnp.where(even, g, roll(g, 1)))
    pack_face(face, zs.at[1])

    conv_rows(fine, w_ff[...], v_f, z_f, rows=range(1, 7), cols=(1, 2))
    arrive(sides)
    spread_y_halo(fine, v_f)
    conv_rows(fine, w_ff[...], v_f, z_f, rows=(0, 7))
    conv_rows(fine, w_ff[...], v_f, z_f, rows=range(1, 7), cols=(0, 3))
    up_ends = send_ends(1, ENDS[-2:])
    up_sides = send_sides(1, up_views)
    arrive(forwards)
    columns_f = halo_columns(fine, planes(fine, zr.at[0]))
    fix = correction(w_ff[...], columns_f)
    for y in range(8):
        for x in range(4):
            h, s = act_slope(fixed(fine, fix, z_f, y, x))
            m = (y % 2) * 2 + x % 2
            hid[y // 2, x // 2, m * C : (m + 1) * C, :] = h.astype(BF16)
            slope_f[y, x] = s

    lane = lanes(C)
    near = jnp.zeros((C, Z), F32)
    far = jnp.zeros((C, Z), F32)
    for y in range(4):
        p = dot(w_d[...], pair(hid, y))
        row = []
        for x in range(2):
            part = p[:, x * Z : (x + 1) * Z]
            d, s = act_slope(part[:C] + roll(part[C:], -1))
            slope_d[y, x] = s
            row.append(d)
            spot = coarse.at(y, x)
            near = jnp.where(
                lane // 2 == spot, roll(jnp.where(even, d, roll(d, 1)), 2 * spot + 1), near
            )
            far = jnp.where(lane == 2 * spot + 1, roll(d, 2 * spot - 1), far)
            far = jnp.where(lane == 2 * spot, roll(d, 2 * spot - 124), far)
        both[y + 2, 1] = jnp.where(even, row[0], roll(row[1], 1)).astype(BF16)
    pack_ends(near, far, zs.at[2])
    sides = send_sides(2, down_views)
    ends = send_ends(2, ENDS)

    arrive(up_ends)
    forwards = forward_ends(1)

    def unpack(y, block):
        value = both[y, block]
        moved = roll(value.astype(F32), -1).astype(BF16)
        for x, pencil in ((2 * block, value), (2 * block + 1, moved)):
            for a in range(3):
                if 0 <= x - a < 4:
                    v_e[y, x - a, a * C : (a + 1) * C, :] = pencil

    for y in range(4):
        unpack(y + 2, 1)
    arrive(sides)
    for y in range(8):
        for block in range(3):
            if block != 1 or not 2 <= y < 6:
                unpack(y, block)
    beyond = conv_rows(outer, w_cf[...], v_e, z_e, jnp.zeros((C, Z), F32))
    arrive(ends)
    plane_1, plane_2 = outer_planes(zr.at[2])
    p_1 = dot(w_cf[...], halo_columns(outer, plane_1))
    p_2 = dot(w_cf[...], halo_columns(outer, plane_2))
    columns_c = halo_columns(outer, roll(plane_1, -14))
    fix = jnp.where(odd, p_1[:C], p_1[2 * C :])
    beyond = beyond + p_1[C : 2 * C] + jnp.where(odd, p_2[:C], p_2[2 * C :])
    arrive(up_sides)
    face = jnp.zeros((C, Z), F32)
    for y in range(6):
        for x in range(4):
            h, s = act_slope(fixed(outer, fix, z_e, y, x))
            own = 1 <= y < 5 and 1 <= x < 3
            up = up_grad[y - 1, x - 1] if own else up_ext[y, x].astype(F32)
            g = jnp.where(even, up * s, 0.0).astype(BF16).astype(F32)
            for a in range(3):
                if 0 <= x - a < 2:
                    g_c[y, x - a, a * C : (a + 1) * C, :] = g.astype(BF16)
            if own:
                h = jnp.where(even, h, 0.0)
                h_two[y - 1, x - 1] = jnp.concatenate([h, roll(h, 1)], axis=0).astype(BF16)
                shifted_c[y - 1, x - 1] = taps_along_z(coarse, g)
                face = add_face(coarse, face, y - 1, x - 1, jnp.where(even, g, roll(g, 1)))
    arrive(forwards)
    g_plane = planes(coarse, zr.at[1]) * act_slope(beyond)[1]
    g_plane = g_plane.astype(BF16).astype(F32)

    def long(ref):
        return jnp.concatenate([ref[y, x] for y in range(4) for x in range(2)], axis=1)

    def place(ref, row):
        chunk = ref.shape[1]
        return row // chunk, pl.ds(row % chunk, 16), slice(None)

    def store(ref, block, value):
        for at in range(0, C, 16):
            ref[place(ref, block * C + at)] = value[at : at + 16].astype(BF16)

    def pack_sums(sums, ref):
        parts = [sums[b][c * C : (c + 1) * C] for c in range(3) for b in range(3)]
        tails = [part[:, Z:] for part in parts] + [jnp.zeros((C, C), F32)]
        for j, part in enumerate(parts):
            store(ref, j, part[:, :Z])
        for q in range(5):
            store(ref, 9 + q, jnp.concatenate(tails[2 * q : 2 * q + 2], axis=1))
        for block in (18, 19):
            store(ref, block, jnp.zeros((C, Z), F32))

    in_plane = [(0, j, k) for j in range(cy) for k in range(cz) if (j, k) != (0, 0)]
    in_plane.sort(key=lambda d: -min(d[1], cy - d[1]) - min(d[2], cz - d[2]))
    in_line = sorted([(i, 0, 0) for i in range(1, cx)], key=lambda d: -min(d[0], cx - d[0]))
    plane_at = me[1] * cz + me[2]
    voxels = 4 * 8 * Z * cx * cy * cz
    scale = 1.0 / (voxels**0.5)

    def send_sum(src, dst, stage, which, n, d):
        return send(src, dst, sum_send.at[stage, which, n], sum_recv.at[stage, which, n], d)

    def scatter(which, s, ra):
        out = []
        for n, d in enumerate(in_plane):
            there = device(d)
            out.append(send_sum(s.at[there[1] * cz + there[2]], ra.at[n], 0, which, n, d))
        return out

    def along(which, s, ra, rb, waits):
        arrive(waits)
        total = s[plane_at].astype(F32)
        for n in range(len(in_plane)):
            total = total + ra[n].astype(F32)
        rb[me[0]] = total.astype(BF16)
        return [
            send_sum(rb.at[me[0]], rb.at[me[0]], 1, which, n, d) for n, d in enumerate(in_line)
        ]

    def gather(which, rb, rc, waits):
        arrive(waits)
        total = rb[0].astype(F32)
        for n in range(1, cx):
            total = total + rb[n].astype(F32)
        rc[plane_at] = (total * scale).astype(BF16)
        return [
            send_sum(rc.at[plane_at], rc.at[plane_at], 2, which, n, d)
            for n, d in enumerate(in_plane)
        ]

    inner = v_e.at[pl.ds(1, 6), pl.ds(1, 2)]
    pack_sums(filter_sum(coarse, shifted_c, face, inner, columns_c), s_a)
    p = dot_nt(long(cot), long(h_two))
    for m in range(4):
        store(s_a, 14 + m, p[m * C : (m + 1) * C])
    waits_a = scatter(0, s_a, ra_a)

    conv_rows(coarse, w_cb[...], g_c, z_c)
    fix = correction(w_cb[...], halo_columns(coarse, g_plane))
    for y in range(4):
        for x in range(2):
            g = jnp.where(even, fixed(coarse, fix, z_c, y, x) * slope_d[y, x], 0.0)
            g_two[y, x] = jnp.concatenate([g, roll(g, 1)], axis=0).astype(BF16)

    face = jnp.zeros((C, Z), F32)
    for half in range(4):
        p = dot(w_dt[...], pair(g_two, half))
        for b in range(2):
            y = half * 2 + b
            for x in range(4):
                m = b * 2 + x % 2
                wide = p[m * C : (m + 1) * C, (x // 2) * Z : (x // 2 + 1) * Z]
                c = cot[half, x // 2, m * C : (m + 1) * C, :].astype(F32)
                g = ((c + wide) * slope_f[y, x]).astype(BF16).astype(F32)
                put_own(fine, g_f, y, x, g.astype(BF16))
                shifted_f[y, x] = taps_along_z(fine, g)
                face = add_face(fine, face, y, x, g)
    pack_face(face, zs.at[3])

    pack_sums(filter_sum(fine, shifted_f, face, v_f, columns_f), s_b)
    p = dot_nt(long(g_two), long(hid))
    for c in range(2):
        for b in range(2):
            store(s_b, 14 + c * 2 + b, p[c * C : (c + 1) * C, b * Z : (b + 1) * Z])
    waits_b = scatter(1, s_b, ra_b)
    ends = send_ends(3, ENDS[-2:])
    sides = send_sides(3, fine_views(g_f))

    waits_a = along(0, s_a, ra_a, rb_a, waits_a)
    arrive(ends)
    forwards = forward_ends(3)
    waits_b = along(1, s_b, ra_b, rb_b, waits_b)
    waits_a = gather(0, rb_a, rc_a, waits_a)
    arrive(sides)
    spread_y_halo(fine, g_f)
    conv_rows(fine, w_fb[...], g_f, z_f)
    waits_b = gather(1, rb_b, rc_b, waits_b)
    arrive(forwards)
    fix = correction(w_fb[...], halo_columns(fine, planes(fine, zr.at[3])))
    for x in range(4):
        for y in range(8):
            turn[x, pl.ds(y, C, stride=8), :] = fixed(fine, fix, z_f, y, x)
        out_ref[:, x] = turn[x].reshape(C, 8, Z).astype(BF16)
    arrive(waits_a)
    a_ref[...] = rc_a[...]
    arrive(waits_b)
    b_ref[...] = rc_b[...]
    for copy in started:
        copy.wait_send()


def finish(
    field_ref, a_ref, b_ref,
    out_hbm, of_hbm, od_hbm, oc_hbm, ou_hbm,
    of_ref, od_ref, oc_ref, ou_ref,
    sems,
):
    copies = []

    def write(src, dst):
        copy = pltpu.make_async_copy(src, dst, sems.at[len(copies)])
        copy.start()
        copies.append(copy)

    write(field_ref, out_hbm)

    def load(ref, block):
        rows = []
        for at in range(block * C, (block + 1) * C, 16):
            rows.append(ref[at // ref.shape[1], pl.ds(at % ref.shape[1], 16), :])
        return jnp.concatenate(rows, axis=0).astype(F32)

    def unpack_sums(ref, o_ref):
        for block in range(14):
            value = load(ref, block)
            for half in range(2):
                j, a = (block, half) if block < 9 else (2 * (block - 9) + half, 2)
                if j < 9:
                    o_ref[a, j % 3, j // 3] = value[:, half * C : (half + 1) * C]

    unpack_sums(a_ref, oc_ref)
    write(oc_ref, oc_hbm)
    unpack_sums(b_ref, of_ref)
    write(of_ref, of_hbm)
    for m in range(4):
        value = load(a_ref, 14 + m)
        for c in range(2):
            ou_ref[m % 2, m // 2, c] = value[:, c * C : (c + 1) * C]
    write(ou_ref, ou_hbm)
    for c in range(2):
        for b in range(2):
            value = load(b_ref, 14 + c * 2 + b)
            for a in range(2):
                od_ref[a, b, c] = value[:, a * C : (a + 1) * C]
    write(od_ref, od_hbm)
    for copy in copies:
        copy.wait()


def solution(mesh):
    sizes = (mesh.shape["gx"], mesh.shape["gy"], mesh.shape["gz"])
    cx, cy, cz = sizes
    plane = cy * cz
    rows_a, rows_b = 20 * C // plane, 20 * C // plane

    def step(field, cotangent, w_fine, w_down, w_coarse, w_up):
        vmem = pl.BlockSpec(memory_space=pltpu.VMEM)
        hbm = pl.BlockSpec(memory_space=pltpu.HBM)
        three, two = (3, 3, 3, C, C), (2, 2, 2, C, C)
        packed = [jax.ShapeDtypeStruct((plane, rows, Z), BF16) for rows in (rows_a, rows_b)]
        whole = jax.ShapeDtypeStruct((C, 4, 8, Z), BF16)
        inputs = [
            pltpu.with_memory_space_constraint(v, pltpu.HBM)
            for v in (field, cotangent, w_fine, w_down, w_coarse, w_up)
        ]
        grad, sums_a, sums_b = pl.pallas_call(
            functools.partial(kernel, sizes),
            out_shape=[whole, *packed],
            in_specs=[hbm] * 6,
            out_specs=[vmem] * 3,
            scratch_shapes=[
                pltpu.VMEM((C, 4, 8, Z), BF16),
                pltpu.VMEM((C, 4, 8, Z), BF16),
                pltpu.VMEM(three, BF16),
                pltpu.VMEM(two, BF16),
                pltpu.VMEM(three, BF16),
                pltpu.VMEM(two, BF16),
                pltpu.VMEM((3 * C, 9 * C), BF16),
                pltpu.VMEM((3 * C, 9 * C), BF16),
                pltpu.VMEM((3 * C, 9 * C), BF16),
                pltpu.VMEM((3 * C, 9 * C), BF16),
                pltpu.VMEM((2 * C, 4 * C), BF16),
                pltpu.VMEM((4 * C, 2 * C), BF16),
                pltpu.VMEM((2 * C, 4 * C), BF16),
                pltpu.VMEM((10, 4, 3 * C, Z), BF16),
                pltpu.VMEM((8, 4, 3 * C, Z), BF16),
                pltpu.VMEM((6, 2, 3 * C, Z), BF16),
                pltpu.VMEM((10, 4, 3 * C, Z), BF16),
                pltpu.VMEM((8, 3, C, Z), BF16),
                pltpu.VMEM((6, 4, C, Z), BF16),
                pltpu.VMEM((4, 2, C // 2, Z), BF16),
                pltpu.VMEM((4, 9, 2, C // 2, Z), BF16),
                pltpu.VMEM((4, 8 * C, Z), F32),
                pltpu.VMEM((4, 2, 4 * C, Z), BF16),
                pltpu.VMEM((4, 2, 4 * C, Z), BF16),
                pltpu.VMEM((4, 2, C, Z), F32),
                pltpu.VMEM((8, 4, C, Z), F32),
                pltpu.VMEM((4, 2, C, Z), F32),
                pltpu.VMEM((8, 4, 3 * C, Z), BF16),
                pltpu.VMEM((4, 2, 3 * C, Z), BF16),
                pltpu.VMEM((4, 2, 2 * C, Z), BF16),
                pltpu.VMEM((4, 2, 2 * C, Z), BF16),
                pltpu.VMEM((8, 4, C, Z), F32),
                pltpu.VMEM((4, 2, C, Z), F32),
                pltpu.VMEM((6, 4, C, Z), F32),
                pltpu.VMEM((plane, rows_a, Z), BF16),
                pltpu.VMEM((plane, rows_b, Z), BF16),
                pltpu.VMEM((plane - 1, rows_a, Z), BF16),
                pltpu.VMEM((plane - 1, rows_b, Z), BF16),
                pltpu.VMEM((cx, rows_a, Z), BF16),
                pltpu.VMEM((cx, rows_b, Z), BF16),
                pltpu.VMEM((plane, rows_a, Z), BF16),
                pltpu.VMEM((plane, rows_b, Z), BF16),
                pltpu.SemaphoreType.DMA((9,)),
                pltpu.SemaphoreType.DMA((4, 8)),
                pltpu.SemaphoreType.DMA((4, 8)),
                pltpu.SemaphoreType.DMA((4, 18)),
                pltpu.SemaphoreType.DMA((4, 18)),
                pltpu.SemaphoreType.DMA((3, 2, 15)),
                pltpu.SemaphoreType.DMA((3, 2, 15)),
            ],
            compiler_params=pltpu.CompilerParams(
                collective_id=0, has_side_effects=True, vmem_limit_bytes=48 * 1024 * 1024
            ),
        )(*inputs)
        return pl.pallas_call(
            finish,
            out_shape=[whole]
            + [jax.ShapeDtypeStruct(s, F32) for s in (three, two, three, two)],
            in_specs=[vmem] * 3,
            out_specs=[hbm] * 5,
            scratch_shapes=[pltpu.VMEM(s, F32) for s in (three, two, three, two)]
            + [pltpu.SemaphoreType.DMA((5,))],
            compiler_params=pltpu.CompilerParams(vmem_limit_bytes=32 * 1024 * 1024),
        )(grad, sums_a, sums_b)

    return jax.shard_map(
        step,
        mesh=mesh,
        in_specs=(P(None, "gx", "gy", "gz"), P(None, "gx", "gy", "gz"), P(), P(), P(), P()),
        out_specs=(P(None, "gx", "gy", "gz"), P(), P(), P(), P()),
        check_vma=False,
    )
```

profile of v0, /device:TPU:1, one launch (start us, length us, event | category | flops | bytes accessed | tf_op | source)
XLA Modules:
  0.0 53.4 jit_solution(11113494043168084225)
XLA Ops:
  0.6 51.1 %shard_map.101 = (bf16[64,4,8,128]{3,2,1,0:T(8,128)(2,1)S(1)}, bf16[16,80,128]{2,1,0:T(8,128)(2,1)S(1)}, bf16[16,80,128]{2,1,0:T(8,128)(2,1)S(1)}) custom-call(bf16[64,4,8,128]{3,2,1,0:T(8,128)(2,1)} %field_hbm.1, bf16[64,4,8,128]{3,2,1,0:T(8,128)(2,1)} %cot_hbm.1, bf16[3,3,3,64,64]{4,3,2,1,0:T(8,128)(2,1)} %wf_hbm.1, bf16[2,2,2,64,64]{4,3,2,1,0:T(8,128)(2,1)} %wd_hbm.1, ...), custom_call_target="tpu_custom_call" | custom-call | tf_op jit(solution)/shard_map/pallas_call | solution.py:666
  51.7 1.6 %shard_map.102 = (bf16[64,4,8,128]{3,2,1,0:T(8,128)(2,1)}, f32[3,3,3,64,64]{4,3,2,1,0:T(8,128)}, f32[2,2,2,64,64]{4,3,2,1,0:T(8,128)}, f32[3,3,3,64,64]{4,3,2,1,0:T(8,128)}, f32[2,2,2,64,64]{4,3,2,1,0:T(8,128)}) custom-call(bf16[64,4,8,128]{3,2,1,0:T(8,128)(2,1)S(1)} %get-tuple-element.8.field_ref, bf16[16,80,128]{2,1,0:T(8,128)(2,1)S(1)} %get-tuple-element.9.a_ref, ...), custom_call_target="tpu_custom_call" | custom-call | tf_op jit(solution)/shard_map/pallas_call | solution.py:726
where the time goes:
time: 53.6 us; the launch traced here: 53.4 us
  Pallas kernels  52.6 us (98%)
  between operations  0.8 us (1%)
    pallas_call x1, Pallas kernels, step(): pl.pallas_call(functools.partial(kernel, sizes), out_shape=[whole, *packe...  51.1 us
    pallas_call x1, Pallas kernels, step(): pl.pallas_call(finish, out_shape=[whole] + [jax.ShapeDtypeStruct(s, F32)...  1.59 us

commit v1 on v0

--- a/solution.py
+++ b/solution.py
@@ -572,8 +572,8 @@
     for c in range(2):
         for b in range(2):
             store(s_b, 14 + c * 2 + b, p[c * C : (c + 1) * C, b * Z : (b + 1) * Z])
+    ends = send_ends(3, ENDS[-2:])
     waits_b = scatter(1, s_b, ra_b)
-    ends = send_ends(3, ENDS[-2:])
     sides = send_sides(3, fine_views(g_f))
 
     waits_a = along(0, s_a, ra_a, rb_a, waits_a)

time: 53.6 us -> 53.4 us (level)
  no operation moved by 1% of the time
where the time goes in v1:
time: 53.4 us; the launch traced here: 53.2 us
  Pallas kernels  52.4 us (98%)
  between operations  0.8 us (1%)
    pallas_call x1, Pallas kernels, step(): pl.pallas_call(functools.partial(kernel, sizes), out_shape=[whole, *packe...  50.8 us
    pallas_call x1, Pallas kernels, step(): pl.pallas_call(finish, out_shape=[whole] + [jax.ShapeDtypeStruct(s, F32)...  1.59 us

profile of v1, /device:TPU:1, one launch (start us, length us, event | category | flops | bytes accessed | tf_op | source)
XLA Modules:
  0.0 53.2 jit_solution(2065881316781135492)
XLA Ops:
  0.6 50.8 %shard_map.101 = (bf16[64,4,8,128]{3,2,1,0:T(8,128)(2,1)S(1)}, bf16[16,80,128]{2,1,0:T(8,128)(2,1)S(1)}, bf16[16,80,128]{2,1,0:T(8,128)(2,1)S(1)}) custom-call(bf16[64,4,8,128]{3,2,1,0:T(8,128)(2,1)} %field_hbm.1, bf16[64,4,8,128]{3,2,1,0:T(8,128)(2,1)} %cot_hbm.1, bf16[3,3,3,64,64]{4,3,2,1,0:T(8,128)(2,1)} %wf_hbm.1, bf16[2,2,2,64,64]{4,3,2,1,0:T(8,128)(2,1)} %wd_hbm.1, ...), custom_call_target="tpu_custom_call" | custom-call | tf_op jit(solution)/shard_map/pallas_call | solution.py:666
  51.5 1.6 %shard_map.102 = (bf16[64,4,8,128]{3,2,1,0:T(8,128)(2,1)}, f32[3,3,3,64,64]{4,3,2,1,0:T(8,128)}, f32[2,2,2,64,64]{4,3,2,1,0:T(8,128)}, f32[3,3,3,64,64]{4,3,2,1,0:T(8,128)}, f32[2,2,2,64,64]{4,3,2,1,0:T(8,128)}) custom-call(bf16[64,4,8,128]{3,2,1,0:T(8,128)(2,1)S(1)} %get-tuple-element.8.field_ref, bf16[16,80,128]{2,1,0:T(8,128)(2,1)S(1)} %get-tuple-element.9.a_ref, ...), custom_call_target="tpu_custom_call" | custom-call | tf_op jit(solution)/shard_map/pallas_call | solution.py:726
